TPU v7x, 32 devices: a whole 2x2x4 slice. The times are simulated.
32 devices in a mesh: rows: 8 (over z, y), pair: 4 (over x, core).
Axes of the slice: x: 2, y: 2, z: 4, core: 2. Of those that a mesh axis runs over, the one named last changes fastest.
Arguments:
- a_tiles: bfloat16 [2048, 8, 4096], P(('rows', 'pair')), may hold values from -2.09375 to 2.09375
- p_tiles: bfloat16 [2048, 4096], P(('rows', 'pair')), may hold values from -0.75 to 0.75
- a_cols: int32 [2048, 8], P(('rows', 'pair')), may hold values from 0 to 2047, as said below
- tile_group: int32 [2048, 8], P(('rows', 'pair')), may hold values from 0 to 1
- coarse_slots: int32 [2048, 2], P(('rows', 'pair')), may hold values from 0 to 15
- aggregate: int32 [2048], P(('rows', 'pair')), may hold values from 0 to 127, as said below
Outputs:
- coarse_tiles: float32 [128, 16, 4096], P(('rows', 'pair'))
Inputs may be any that keep to these rules, and one draw needn't show every extreme that they name: `a_cols`: each operator tile's column block lies within 2 block rows of its own block row. `aggregate`: coarse block rows come in groups of 16 consecutive ones, group g held by index g of rows; the fine block rows of one device name at most 16 rows of one group, and one group, drawn from the seed, gets exactly 16 from every device.
All inputs are finite; a program needn't handle non-finite values.
Results may differ from a plain program's by a relative error of at most 0.0041.
Values may be sent and summed in bfloat16 or wider, within the bound.
A program may use at most 128 MiB of HBM per device.

v0:
```python
import jax
import jax.numpy as jnp
from jax import lax
from jax.sharding import PartitionSpec as P

BLK = 64
KA = 8
KS = 2
KC = 16
HB = 2
RATIO = 16


def extended(array, sides, width):
    for axis, dim in sides:
        devices, length = (lax.axis_size(axis), array.shape[dim])
        up = [(i, (i + 1) % devices) for i in range(devices - 1)]
        down = [(j, i) for i, j in up]
        last = lax.slice_in_dim(array, length - width, length, axis=dim)
        initial = lax.slice_in_dim(array, 0, width, axis=dim)
        before = lax.ppermute(last, axis, up)
        after = lax.ppermute(initial, axis, down)
        array = jnp.concatenate([before, array, after], axis=dim)
    return array


def group_sums(products, tile_picks):
    selector = (tile_picks[..., None] == jnp.arange(KS, dtype=jnp.int32)).astype(jnp.bfloat16)
    return jnp.einsum(
        "...ks,...kf->...sf", selector, products, preferred_element_type=jnp.float32
    ).astype(jnp.bfloat16)


def contract(prolong, slot_sums):
    prolong_blocks = prolong.reshape(prolong.shape[:-1] + (BLK, BLK))
    sum_blocks = slot_sums.reshape(slot_sums.shape[:-1] + (BLK, BLK))
    result = jnp.einsum(
        "...ji,...sjc->...sic", prolong_blocks, sum_blocks, preferred_element_type=jnp.float32
    )
    return result.reshape(slot_sums.shape)


def body(a_tiles, p_tiles, a_cols, tile_group, coarse_slots, aggregate):
    fine_rows = a_tiles.shape[0]
    tile_width = p_tiles.shape[1]
    rows_count = lax.axis_size("rows")
    pair_count = lax.axis_size("pair")
    device = lax.axis_index("rows") * pair_count + lax.axis_index("pair")
    padded = extended(p_tiles, ((("rows", "pair"), 0),), HB)
    local_cols = a_cols - device * fine_rows + HB
    near_tiles = padded[local_cols].reshape(fine_rows, KA, BLK, BLK)
    a_blocks = a_tiles.reshape(fine_rows, KA, BLK, BLK)
    products = jnp.einsum(
        "tkab,tkbc->tkac", a_blocks, near_tiles, preferred_element_type=jnp.float32
    )
    products = products.astype(jnp.bfloat16).reshape(fine_rows, KA, tile_width)
    slot_sums = group_sums(products, tile_group)
    group_size = fine_rows // RATIO * pair_count
    capacity = 2 * fine_rows // rows_count
    dest_group = aggregate // group_size
    local_rows = aggregate - dest_group * group_size
    targets = local_rows[:, None] * KC + coarse_slots
    dest_onehot = (dest_group[:, None] == jnp.arange(rows_count, dtype=jnp.int32)[None, :]).astype(
        jnp.int32
    )
    rank_in = jnp.sum(jnp.cumsum(dest_onehot, axis=0) * dest_onehot, axis=1) - 1
    position = dest_group * capacity + rank_in

    def place_rows(values):
        buffer = jnp.zeros((rows_count * capacity,) + values.shape[1:], values.dtype)
        buffer = buffer.at[position].set(values)
        return buffer.reshape((rows_count, capacity) + values.shape[1:])

    got_sums = lax.all_to_all(
        place_rows(slot_sums), "rows", split_axis=0, concat_axis=0, tiled=True
    )
    got_prolong = lax.all_to_all(
        place_rows(p_tiles), "rows", split_axis=0, concat_axis=0, tiled=True
    )
    got_targets = lax.all_to_all(
        place_rows(targets), "rows", split_axis=0, concat_axis=0, tiled=True
    )
    coarse_terms = contract(got_prolong, got_sums)
    coarse_panel = jax.ops.segment_sum(
        coarse_terms.reshape(-1, tile_width), got_targets.reshape(-1), num_segments=group_size * KC
    )
    coarse_panel = coarse_panel.reshape(group_size, KC, tile_width)
    return lax.psum_scatter(coarse_panel, "pair", scatter_dimension=0, tiled=True)


def solution(mesh):
    return jax.shard_map(
        body,
        mesh=mesh,
        in_specs=(
            P(("rows", "pair"), None, None),
            P(("rows", "pair"), None),
            P(("rows", "pair"), None),
            P(("rows", "pair"), None),
            P(("rows", "pair"), None),
            P(("rows", "pair")),
        ),
        out_specs=P(("rows", "pair"), None, None),
        check_vma=False,
    )
```

profile of v0, /device:TPU:0, one launch (start us, length us, event | category | flops | bytes accessed | tf_op | source)
XLA Modules:
  0.0 254.8 jit_solution(1968341022793451442)
XLA Ops:
  6.5 0.9 fusion.16
  7.4 2.4 collective-permute-start
  9.8 1.3 collective-permute-start.1
  11.1 0.7 subtract_multiply_fusion
  11.8 0.1 fusion.13
  11.8 0.1 reduce_window_sum.11
  11.9 0.2 select_reduce_fusion
  12.1 0.7 broadcast_add_fusion
  12.8 0.1 copy.34
  12.9 0.8 scatter_custom_fusion
  13.7 0.7 copy.35
  14.4 10.1 %all-to-all-start = ((s32[8,16,2]{1,2,0:T(2,128)}), s32[8,16,2]{1,2,0:T(2,128)S(1)}, u32[]{:S(2)}, u32[]{:S(2)}) async-start(s32[8,16,2]{1,2,0:T(2,128)} %copy.35), calls=%async_computation | async-start | bytes 16384 | tf_op jit(solution)/shard_map/all_to_all | solution.py:80
  24.5 0.8 copy.38
  25.3 0.1 reshape.42
  25.4 0.0 copy-start.1
  25.4 0.0 copy-start
  25.4 12.6 %reshape.33 = bf16[64,8,64,64]{3,2,1,0:T(8,128)(2,1)} reshape(bf16[64,8,4096]{2,1,0:T(8,128)(2,1)} %param.6) | data formatting | bytes 8388608 | tf_op jit(solution)/shard_map/reshape | solution.py:52
  38.0 0.0 copy-done.1
  38.0 0.1 copy.37
  38.1 2.5 scatter_custom_fusion.2
  40.6 0.0 collective-permute-done
  40.6 0.0 collective-permute-done.1
  40.6 0.2 pad_maximum_fusion
  40.8 4.4 %gather_fusion = bf16[512,4096]{1,0:T(8,128)(2,1)} fusion(bf16[68,4096]{1,0:T(8,128)(2,1)S(1)} %pad_maximum_fusion, s32[1024]{0:T(1024)S(1)} %pad_clamp_fusion), kind=kCustom, calls=%fused_computation | custom fusion | bytes 8390656 | tf_op jit(solution)/shard_map/gather | solution.py:51
  45.1 12.5 %reshape.32 = bf16[64,8,64,64]{3,2,1,0:T(8,128)(2,1)} reshape(bf16[512,4096]{1,0:T(8,128)(2,1)} %gather_fusion) | data formatting | bytes 8388608 | tf_op jit(solution)/shard_map/reshape | solution.py:51
  57.7 0.0 all-to-all-done
  57.7 6.0 %all-to-all-start.2 = ((bf16[8,16,4096]{2,1,0:T(8,128)(2,1)}), bf16[8,16,4096]{2,1,0:T(8,128)(2,1)S(1)}, u32[]{:S(2)}, u32[]{:S(2)}) async-start(bf16[8,16,4096]{2,1,0:T(8,128)(2,1)} %bitcast.3), calls=%async_computation.2 | async-start | bytes 2097152 | tf_op jit(solution)/shard_map/all_to_all | solution.py:77
  63.7 10.2 %convert_bitcast_fusion = bf16[64,8,64,64]{2,3,1,0:T(8,128)(2,1)} fusion(bf16[64,8,64,64]{3,2,1,0:T(8,128)(2,1)} %reshape.32, bf16[64,8,64,64]{3,2,1,0:T(8,128)(2,1)} %reshape.33), kind=kOutput, calls=%fused_computation.5 | convolution fusion | flops 270532608 | bytes 12582912 | tf_op jit(solution)/shard_map/tkab,tkbc->tkac/dot_general | solution.py:53
  73.9 11.9 %copy.40 = bf16[64,8,64,64]{3,2,1,0:T(8,128)(2,1)} copy(bf16[64,8,64,64]{2,3,1,0:T(8,128)(2,1)} %convert_bitcast_fusion) | data formatting | bytes 8388608 | tf_op jit(solution)/shard_map/convert_element_type | solution.py:56
  85.8 12.1 %reshape.34 = bf16[64,8,4096]{2,1,0:T(8,128)(2,1)} reshape(bf16[64,8,64,64]{3,2,1,0:T(8,128)(2,1)} %copy.40) | data formatting | bytes 8388608 | tf_op jit(solution)/shard_map/reshape | solution.py:56
  97.9 4.4 %convolution_convert_fusion = bf16[64,2,4096]{2,1,0:T(2,128)(2,1)} fusion(bf16[64,8,4096]{2,1,0:T(8,128)(2,1)} %reshape.34, s32[64,8]{1,0:T(8,128)S(1)} %copy.37), kind=kOutput, calls=%fused_computation.6 | convolution fusion | flops 8913920 | bytes 5244928 | tf_op jit(solution)/shard_map/...ks,...kf->...sf/dot_general | solution.py:29
  102.3 2.1 broadcast_in_dim.28
  104.4 6.3 %scatter_fusion = bf16[128,2,4096]{2,1,0:T(2,128)(2,1)S(1)} fusion(bf16[128,2,4096]{2,1,0:T(2,128)(2,1)S(1)} %broadcast_in_dim.28, s32[64]{0:T(128)S(1)} %compare_select_fusion.1, bf16[64,2,4096]{2,1,0:T(2,128)(2,1)} %convolution_convert_fusion), kind=kCustom, calls=%fused_computation.2 | custom fusion | bytes 3145984 | tf_op jit(solution)/shard_map/scatter | solution.py:71
  110.6 2.7 %copy.42 = bf16[8,16,2,4096]{3,1,2,0:T(8,128)(2,1)} copy(bf16[8,16,2,4096]{3,2,1,0:T(2,128)(2,1)S(1)} %bitcast.23) | data formatting | bytes 4194304 | tf_op jit(solution)/shard_map/reshape | solution.py:72
  113.3 0.0 all-to-all-done.2
  113.3 6.0 %all-to-all-start.1 = ((bf16[8,16,2,4096]{3,1,2,0:T(8,128)(2,1)}), bf16[8,16,2,4096]{3,1,2,0:T(8,128)(2,1)S(1)}, u32[]{:S(2)}, u32[]{:S(2)}) async-start(bf16[8,16,2,4096]{3,1,2,0:T(8,128)(2,1)} %copy.42), calls=%async_computation.1 | async-start | bytes 4194304 | tf_op jit(solution)/shard_map/all_to_all | solution.py:74
  119.3 0.3 reduce-scatter.2.cloned.1.call-start
  119.6 0.1 copy.36
  119.7 0.1 reshape.74
  119.8 3.3 %reshape.87 = bf16[8,16,64,64,1]{3,2,1,0,4:T(8,128)(2,1)} reshape(bf16[8,16,4096]{2,1,0:T(8,128)(2,1)S(1)} %all-to-all-done.2) | data formatting | bytes 2097152 | tf_op jit(solution)/shard_map/reshape | solution.py:35
  123.1 42.7 %all-to-all-done.1 = bf16[8,16,2,4096]{3,1,2,0:T(8,128)(2,1)S(1)} async-done(((bf16[8,16,2,4096]{3,1,2,0:T(8,128)(2,1)}), bf16[8,16,2,4096]{3,1,2,0:T(8,128)(2,1)S(1)}, u32[]{:S(2)}, u32[]{:S(2)}) %all-to-all-start.1) | async-done | bytes 2097184 | tf_op jit(solution)/shard_map/all_to_all | solution.py:74
  165.8 5.5 %reshape.36 = bf16[8,16,2,64,64]{4,3,1,2,0:T(8,128)(2,1)} reshape(bf16[8,16,2,4096]{3,1,2,0:T(8,128)(2,1)S(1)} %all-to-all-done.1) | data formatting | bytes 4194304 | tf_op jit(solution)/shard_map/reshape | solution.py:36
  171.3 7.4 %fusion.2 = f32[8,16,2,64,64]{3,4,2,1,0:T(8,128)} fusion(bf16[8,16,2,64,64]{4,3,1,2,0:T(8,128)(2,1)} %reshape.36, bf16[8,16,64,64,1]{3,2,1,0,4:T(8,128)(2,1)} %reshape.87), kind=kOutput, calls=%fused_computation.9 | convolution fusion | flops 134217728 | bytes 7340032 | tf_op jit(solution)/shard_map/...ji,...sjc->...sic/dot_general | solution.py:37
  178.7 9.1 %copy.44 = f32[8,16,2,64,64]{4,3,2,1,0:T(8,128)} copy(f32[8,16,2,64,64]{3,4,2,1,0:T(8,128)} %fusion.2) | data formatting | bytes 8388608 | tf_op jit(solution)/shard_map/...ji,...sjc->...sic/transpose | solution.py:37
  187.8 7.9 %reshape.76 = f32[256,4096]{1,0:T(8,128)} reshape(f32[8,16,2,64,64]{4,3,2,1,0:T(8,128)} %copy.44) | data formatting | bytes 8388608 | tf_op jit(solution)/shard_map/reshape;reshape | solution.py:85
  195.7 9.7 %scatter_custom_fusion.3 = f32[256,4096]{1,0:T(8,128)} fusion(s32[256]{0:T(256)S(1)} %reshape.74, f32[256,4096]{1,0:T(8,128)} %reshape.76, f32[]{:T(128)} %constant.16.clone.1), kind=kCustom, calls=%fused_computation.11 | custom fusion | flops 1048576 | bytes 4194816 | tf_op jit(solution)/shard_map/scatter-add | solution.py:84
  205.4 0.0 reduce-scatter.2.cloned.1.call-update
  205.4 42.5 %reduce-scatter.2.cloned.1.call-done = f32[4,16,4096]{2,1,0:T(8,128)} async-done(((f32[16,16,4096]{2,1,0:T(8,128)}), f32[4,16,4096]{2,1,0:T(8,128)}) %reduce-scatter.2.cloned.1.call-update) | async-done | bytes 1048592 | tf_op jit(solution)/shard_map/reduce_scatter | solution.py:88
  (4 shorter events, 0.0 us)
Async XLA Ops:
  7.4 33.2 %collective-permute-start = (bf16[2,4096]{1,0:T(2,128)(2,1)S(1)}, bf16[2,4096]{1,0:T(2,128)(2,1)S(1)}, u32[]{:S(2)}, u32[]{:S(2)}) collective-permute-start(bf16[2,4096]{1,0:T(2,128)(2,1)S(1)} %get-tuple-element.7), channel_id=1, source_target_pairs={{0,1},{1,2},{2,3},{3,4},{4,5},{5,6},{6,7},{7,8},{8,9},{9,10},{10,1... | collective-permute-start | bytes 49160 | tf_op jit(solution)/shard_map/ppermute | solution.py:21
  9.8 30.8 %collective-permute-start.1 = (bf16[2,4096]{1,0:T(2,128)(2,1)S(1)}, bf16[2,4096]{1,0:T(2,128)(2,1)S(1)}, u32[]{:S(2)}, u32[]{:S(2)}) collective-permute-start(bf16[2,4096]{1,0:T(2,128)(2,1)S(1)} %get-tuple-element.8), channel_id=1, source_target_pairs={{1,0},{2,1},{3,2},{4,3},{5,4},{6,5},{7,6},{8,7},{9,8},{10,9},{11,1... | collective-permute-start | bytes 49160 | tf_op jit(solution)/shard_map/ppermute | solution.py:22
  14.4 43.3 %all-to-all-start = ((s32[8,16,2]{1,2,0:T(2,128)}), s32[8,16,2]{1,2,0:T(2,128)S(1)}, u32[]{:S(2)}, u32[]{:S(2)}) async-start(s32[8,16,2]{1,2,0:T(2,128)} %copy.35), calls=%async_computation | async-start | bytes 16384 | tf_op jit(solution)/shard_map/all_to_all | solution.py:80
  25.4 12.7 %copy-start.1 = (s32[64,8]{0,1:T(8,128)S(1)}, s32[64,8]{0,1:T(8,128)}, u32[]{:S(2)}) copy-start(s32[64,8]{0,1:T(8,128)} %param.9) | copy-start | bytes 6148
  25.4 12.7 %copy-start = (bf16[64,4096]{1,0:T(8,128)(2,1)S(1)}, bf16[64,4096]{1,0:T(8,128)(2,1)}, u32[]{:S(2)}) copy-start(bf16[64,4096]{1,0:T(8,128)(2,1)} %param.7) | copy-start | bytes 1572868
  57.7 55.6 %all-to-all-start.2 = ((bf16[8,16,4096]{2,1,0:T(8,128)(2,1)}), bf16[8,16,4096]{2,1,0:T(8,128)(2,1)S(1)}, u32[]{:S(2)}, u32[]{:S(2)}) async-start(bf16[8,16,4096]{2,1,0:T(8,128)(2,1)} %bitcast.3), calls=%async_computation.2 | async-start | bytes 2097152 | tf_op jit(solution)/shard_map/all_to_all | solution.py:77
  113.3 52.5 %all-to-all-start.1 = ((bf16[8,16,2,4096]{3,1,2,0:T(8,128)(2,1)}), bf16[8,16,2,4096]{3,1,2,0:T(8,128)(2,1)S(1)}, u32[]{:S(2)}, u32[]{:S(2)}) async-start(bf16[8,16,2,4096]{3,1,2,0:T(8,128)(2,1)} %copy.42), calls=%async_computation.1 | async-start | bytes 4194304 | tf_op jit(solution)/shard_map/all_to_all | solution.py:74
  119.3 128.6 %reduce-scatter.2.cloned.1.call-start = ((), (), s32[]{:S(2)}) async-start(), calls=%async_computation.4 | async-start | bytes 5242880 | tf_op jit(solution)/shard_map/reduce_scatter | solution.py:88
Sparse Core Ops, SparseCore 0:
  205.5 42.3 reduce-scatter.1
where the time goes:
time: 257 us; the launch traced here: 255 us
  local copies, waits for them, and re-layouts  96.5 us (38%)
  waiting for transfers between devices  85.2 us (33%)
  starting transfers between devices  26 us (10%)
  matrix products  22 us (9%)
  between operations  13.5 us (5%)
  other arithmetic  11.6 us (5%)
    all_to_all x1, waiting for transfers between devices, body(): lax.all_to_all(place_rows(slot_sums), 'rows', split_axis=0, concat_axis=0...  42.7 us
    reduce_scatter x1, waiting for transfers between devices, body(): lax.psum_scatter(coarse_panel, 'pair', scatter_dimension=0, tiled=True)  42.5 us
    reshape x1, local copies, waits for them, and re-layouts, body(): a_blocks = a_tiles.reshape(fine_rows, KA, BLK, BLK)  12.6 us
    reshape x1, local copies, waits for them, and re-layouts, body(): near_tiles = padded[local_cols].reshape(fine_rows, KA, BLK, BLK)  12.5 us
    reshape x1, local copies, waits for them, and re-layouts, body(): products = products.astype(jnp.bfloat16).reshape(fine_rows, KA, tile_width)  12.1 us
    convert_element_type x1, local copies, waits for them, and re-layouts, body(): products = products.astype(jnp.bfloat16).reshape(fine_rows, KA, tile_width)  11.9 us
    dot_general x1, matrix products, body(): jnp.einsum('tkab,tkbc->tkac', a_blocks, near_tiles, preferred_element_typ...  10.2 us
    all_to_all x1, starting transfers between devices, body(): lax.all_to_all(place_rows(targets), 'rows', split_axis=0, concat_axis=0,...  10.1 us
  transfers between devices with their start and end apart: 6, of which 2 were waited for; matrix products, arithmetic and copies ran while one was open for 35% of the time, Pallas kernels for 0%

commit v1 on v0

v1 whole, which is shorter than its diff:
```python
import functools

import jax
import jax.numpy as jnp
from jax import lax
from jax.experimental import pallas as pl
from jax.experimental.pallas import tpu as pltpu
from jax.sharding import PartitionSpec as P

BLK = 64
KA = 8
KS = 2
KC = 16
HB = 2
RATIO = 16
LANES = 128
NEAR = 2 * HB + 1
CHUNK = 8
BOTH = ("rows", "pair")


def extended(array, width):
    devices, length = lax.axis_size(BOTH), array.shape[0]
    up = [(i, i + 1) for i in range(devices - 1)]
    down = [(j, i) for i, j in up]
    before = lax.ppermute(array[length - width :], BOTH, up)
    after = lax.ppermute(array[:width], BOTH, down)
    return jnp.concatenate([before, array, after], axis=0)


def iota(shape, dim):
    return lax.broadcasted_iota(jnp.int32, shape, dim)


def terms_kernel(a_ref, p_ref, code_ref, group_ref, out_ref, diag, stage):
    step = pl.program_id(0)
    count = p_ref.shape[0]
    q = BLK // 2

    @pl.when(step == 0)
    def _():
        r, k = iota((LANES, LANES), 0), iota((LANES, LANES), 1)
        want = jnp.where(
            (r // BLK == k // BLK) & (r % BLK == 2 * (k % q) + (k // q) % 2), 1.0, 0.0
        ).astype(jnp.bfloat16)
        low = iota((q, LANES), 1) < BLK

        def one(t, _):
            flat = p_ref[t].astype(jnp.float32)
            turned = pltpu.roll(flat, BLK, 1)
            zero = jnp.zeros_like(flat)
            parts = jnp.concatenate(
                [
                    jnp.where(low, flat, zero),
                    jnp.where(low, turned, zero),
                    jnp.where(low, zero, turned),
                    jnp.where(low, zero, flat),
                ],
                axis=0,
            ).astype(jnp.bfloat16)
            diag[pl.ds(pl.multiple_of(t * LANES, LANES), LANES), :] = jnp.dot(
                want, parts, preferred_element_type=jnp.float32
            ).astype(jnp.bfloat16)
            return 0

        lax.fori_loop(0, count, one, 0, unroll=4)

    eye = jnp.where(iota((LANES, LANES), 0) == iota((LANES, LANES), 1), 1.0, 0.0).astype(
        jnp.bfloat16
    )
    spread = jnp.where(
        iota((q, q * KA), 0) == iota((q, q * KA), 1) // KA, 1.0, 0.0
    ).astype(jnp.bfloat16)
    low = iota((q, LANES), 1) < BLK

    for i in range(CHUNK):
        row = step * CHUNK + i
        code = code_ref[i]
        masks = [code == j for j in range(NEAR)]
        columns = []
        for j in range(NEAR):
            pieces = []
            for c in range(q):
                piece = a_ref[i, :, c * LANES : (c + 1) * LANES].astype(jnp.float32)
                pieces.append(jnp.where(masks[j], piece, 0.0))
            columns.append(jnp.concatenate(pieces, axis=0).astype(jnp.bfloat16))
        left = jnp.concatenate(columns, axis=1)
        near = diag[pl.ds(pl.multiple_of(row * LANES, LANES), NEAR * LANES), :]
        products = jnp.dot(left, near, preferred_element_type=jnp.float32).astype(jnp.bfloat16)
        own = p_ref[row + HB]
        turned = lax.dot_general(
            eye, own, (((1,), (1,)), ((), ())), preferred_element_type=jnp.float32
        ).astype(jnp.bfloat16)
        wide = jnp.dot(turned, spread, preferred_element_type=jnp.float32)
        group = group_ref[i]
        rows = jnp.concatenate(
            [jnp.where(group == s, wide, 0.0) for s in range(KS)], axis=0
        ).astype(jnp.bfloat16)
        full = jnp.dot(rows, products, preferred_element_type=jnp.float32)
        for s in range(KS):
            part = full[s * LANES : (s + 1) * LANES]
            term = jnp.where(low, part[:q], part[3 * q :]) + pltpu.roll(
                jnp.where(low, part[q : 2 * q], part[2 * q : 3 * q]), BLK, 1
            )
            stage[pl.ds(s * CHUNK + i, q, stride=KS * CHUNK), :] = term
    out_ref[...] = stage[...].astype(jnp.bfloat16).reshape(out_ref.shape)


def local_terms(a_tiles, p_tiles, a_cols, tile_group):
    fine_rows = a_tiles.shape[0]
    device = lax.axis_index(BOTH)
    q = BLK // 2
    near_p = extended(p_tiles, HB).reshape(fine_rows + 2 * HB, q, LANES)
    own = device * fine_rows + jnp.arange(fine_rows, dtype=jnp.int32)
    offset = a_cols - own[:, None] + HB
    code = jnp.broadcast_to(offset[:, :, None], (fine_rows, KA, LANES))
    group = jnp.tile(tile_group, (1, q)).reshape(fine_rows, 1, q * KA)
    steps = fine_rows // CHUNK
    return pl.pallas_call(
        terms_kernel,
        grid=(steps,),
        in_specs=[
            pl.BlockSpec((CHUNK, KA, BLK * BLK), lambda g: (g, 0, 0)),
            pl.BlockSpec((fine_rows + 2 * HB, q, LANES), lambda g: (0, 0, 0)),
            pl.BlockSpec((CHUNK, KA, LANES), lambda g: (g, 0, 0)),
            pl.BlockSpec((CHUNK, 1, q * KA), lambda g: (g, 0, 0)),
        ],
        out_specs=pl.BlockSpec((q, KS * CHUNK, LANES), lambda g: (0, g, 0)),
        out_shape=jax.ShapeDtypeStruct((q, fine_rows * KS, LANES), jnp.bfloat16),
        scratch_shapes=[
            pltpu.VMEM(((fine_rows + 2 * HB) * LANES, LANES), jnp.bfloat16),
            pltpu.VMEM((q * KS * CHUNK, LANES), jnp.float32),
        ],
        compiler_params=pltpu.CompilerParams(vmem_limit_bytes=40 * 1024 * 1024),
    )(a_tiles, near_p, code, group)


def in_term_order(values):
    rows = values.shape[0]
    return values.reshape(rows // CHUNK, CHUNK, KS).transpose(0, 2, 1).reshape(rows * KS)


def sum_kernel(tile_rows, target_ref, term_ref, out_ref):
    first = pl.program_id(0) * tile_rows
    tiles = first + iota((tile_rows, target_ref.shape[1]), 0)
    hot = jnp.where(tiles == target_ref[...], 1.0, 0.0).astype(jnp.bfloat16)
    out_ref[...] = jnp.dot(hot, term_ref[...], preferred_element_type=jnp.float32).astype(
        jnp.bfloat16
    )


def sum_terms(targets, terms, tiles):
    tile_rows = 256
    count = terms.shape[0]
    return pl.pallas_call(
        functools.partial(sum_kernel, tile_rows),
        grid=(tiles // tile_rows,),
        in_specs=[
            pl.BlockSpec((1, count), lambda g: (0, 0)),
            pl.BlockSpec((count, LANES), lambda g: (0, 0)),
        ],
        out_specs=pl.BlockSpec((tile_rows, LANES), lambda g: (g, 0)),
        out_shape=jax.ShapeDtypeStruct((tiles, LANES), jnp.bfloat16),
        compiler_params=pltpu.CompilerParams(vmem_limit_bytes=40 * 1024 * 1024),
    )(targets, terms)


def join_kernel(in_ref, out_ref):
    devices, tiles = in_ref.shape[:2]
    low = iota((tiles, LANES), 1) < BLK
    half = devices * BLK
    for m in range(devices // 2):
        one, two = in_ref[2 * m].astype(jnp.float32), in_ref[2 * m + 1].astype(jnp.float32)
        at = m * LANES
        out_ref[:, at : at + LANES] = jnp.where(low, one, pltpu.roll(two, BLK, 1))
        out_ref[:, half + at : half + at + LANES] = jnp.where(low, pltpu.roll(one, BLK, 1), two)


def join(parts):
    devices, tiles, _ = parts.shape
    return pl.pallas_call(
        join_kernel,
        out_shape=jax.ShapeDtypeStruct((tiles, devices * LANES), jnp.float32),
    )(parts)


def routed(terms, coarse_slots, aggregate):
    fine_rows = aggregate.shape[0]
    q = BLK // 2
    width = BLK * BLK
    rows_count, pair_count = lax.axis_size("rows"), lax.axis_size("pair")
    flat = terms.reshape(q, fine_rows // CHUNK, KS, CHUNK, 2, BLK)
    flat = flat.transpose(1, 3, 2, 4, 0, 5).reshape(fine_rows, KS, width)
    group_size = fine_rows // RATIO * pair_count
    capacity = 2 * fine_rows // rows_count
    dest_group = aggregate // group_size
    local_rows = aggregate - dest_group * group_size
    targets = local_rows[:, None] * KC + coarse_slots
    order = jnp.arange(fine_rows)
    same = (dest_group[:, None] == dest_group[None, :]) & (order[None, :] < order[:, None])
    position = dest_group * capacity + jnp.sum(same.astype(jnp.int32), axis=1)

    def exchange(values):
        buffer = jnp.zeros((rows_count * capacity,) + values.shape[1:], values.dtype)
        buffer = buffer.at[position].set(values)
        return lax.all_to_all(buffer, "rows", split_axis=0, concat_axis=0, tiled=True)

    got = exchange(flat).reshape(-1, width).astype(jnp.float32)
    panel = jax.ops.segment_sum(
        got, exchange(targets).reshape(-1), num_segments=group_size * KC
    )
    panel = panel.reshape(group_size, KC, width)
    return lax.psum_scatter(panel, "pair", scatter_dimension=0, tiled=True)


def body(a_tiles, p_tiles, a_cols, tile_group, coarse_slots, aggregate):
    fine_rows, width = p_tiles.shape
    devices = lax.axis_size(BOTH)
    terms = local_terms(a_tiles, p_tiles, a_cols, tile_group)
    if devices * LANES != width:
        return routed(terms, coarse_slots, aggregate)
    tiles = fine_rows // RATIO * KC
    targets = in_term_order(aggregate[:, None] * KC + coarse_slots)
    targets = lax.all_gather(targets, BOTH, axis=0, tiled=True).reshape(1, -1)
    got = lax.all_to_all(terms, BOTH, split_axis=0, concat_axis=0, tiled=True)
    sums = sum_terms(targets, got.reshape(-1, LANES), devices * tiles)
    parts = lax.all_to_all(
        sums.reshape(devices, tiles, LANES), BOTH, split_axis=0, concat_axis=0, tiled=True
    )
    return join(parts).reshape(fine_rows // RATIO, KC, width)


def solution(mesh):
    return jax.shard_map(
        body,
        mesh=mesh,
        in_specs=(
            P(BOTH, None, None),
            P(BOTH, None),
            P(BOTH, None),
            P(BOTH, None),
            P(BOTH, None),
            P(BOTH),
        ),
        out_specs=P(BOTH, None, None),
        check_vma=False,
    )
```

time: 257 us -> 123 us (0.48)
  local copies, waits for them, and re-layouts: 96.5 us -> 3.74 us
  waiting for transfers between devices: 85.2 us -> 2.96 us
  blocking collectives: 0 us -> 69.7 us
  Pallas kernels: 0 us -> 32.2 us
  matrix products: 22 us -> 0 us
  starting transfers between devices: 26 us -> 12.4 us
  between operations: 13.5 us -> 0.15 us
  other arithmetic: 11.6 us -> 1.92 us
    all_gather x0 -> x1, blocking collectives: none -> 51.8 us  [body(): targets = lax.all_gather(targets, BOTH, axis=0, tiled=True).reshape(1, -1)]
    reshape x7 -> x2, local copies, waits for them, and re-layouts: 49.4 us -> 0.12 us  [the longest x1 0.08 us: in_term_order(): values.reshape(rows // CHUNK, CHUNK, KS).transpose(0, 2, 1)]
    all_to_all x3 -> x1, waiting for transfers between devices: 42.7 us -> 0.01 us  [body(): got = lax.all_to_all(terms, BOTH, split_axis=0, concat_axis=0, tiled=True)]
    reduce_scatter x1 -> x0, waiting for transfers between devices: 42.5 us -> none  [body(): lax.psum_scatter(coarse_panel, 'pair', scatter_dimension=0, tiled=True)]
    pallas_call x0 -> x3, Pallas kernels: none -> 32.2 us  [the longest x1 24.3 us: local_terms(): pl.pallas_call(terms_kernel, grid=(steps,), in_specs=[pl.BlockSpec((CHUNK...]
    dot_general x3 -> x0, matrix products: 22 us -> none  [the longest x1 10.2 us: body(): jnp.einsum('tkab,tkbc->tkac', a_blocks, near_tiles, preferred_element_typ...]
    all_to_all x0 -> x1, blocking collectives: none -> 17.9 us  [body(): lax.all_to_all(sums.reshape(devices, tiles, LANES), BOTH, split_axis=0, c...]
    all_to_all x3 -> x1, starting transfers between devices: 22.1 us -> 8.71 us  [body(): got = lax.all_to_all(terms, BOTH, split_axis=0, concat_axis=0, tiled=True)]
  transfers between devices with their start and end apart: 6 -> 3, of which waited for: 2 -> 1; matrix products, arithmetic and copies ran while one was open for 35% -> 1% of each run, Pallas kernels for 0% -> 0%
where the time goes in v1:
time: 123 us
  blocking collectives  69.7 us (57%)
  Pallas kernels  32.2 us (26%)
  starting transfers between devices  12.4 us (10%)
  local copies, waits for them, and re-layouts  3.74 us (3%)
  waiting for transfers between devices  2.96 us (2%)
  other arithmetic  1.92 us (2%)
    all_gather x1, blocking collectives, body(): targets = lax.all_gather(targets, BOTH, axis=0, tiled=True).reshape(1, -1)  51.8 us
    pallas_call x1, Pallas kernels, local_terms(): pl.pallas_call(terms_kernel, grid=(steps,), in_specs=[pl.BlockSpec((CHUNK...  24.3 us
    all_to_all x1, blocking collectives, body(): lax.all_to_all(sums.reshape(devices, tiles, LANES), BOTH, split_axis=0, c...  17.9 us
    all_to_all x1, starting transfers between devices, body(): got = lax.all_to_all(terms, BOTH, split_axis=0, concat_axis=0, tiled=True)  8.71 us
    pallas_call x1, Pallas kernels, sum_terms(): pl.pallas_call(functools.partial(sum_kernel, tile_rows), grid=(tiles // t...  5.61 us
    ppermute x1, waiting for transfers between devices, extended(): after = lax.ppermute(array[:width], BOTH, down)  2.96 us
  transfers between devices with their start and end apart: 3, of which 1 were waited for; matrix products, arithmetic and copies ran while one was open for 1% of the time, Pallas kernels for 0%

profile of v1, /device:TPU:0, one launch (start us, length us, event | category | flops | bytes accessed | tf_op | source)
XLA Modules:
  0.0 123.0 jit_solution(4816601675983302304)
XLA Ops:
  0.0 0.0 copy-start
  0.0 0.9 fusion
  0.9 2.4 %collective-permute-start = (bf16[2,4096]{1,0:T(2,128)(2,1)S(1)}, bf16[2,4096]{1,0:T(2,128)(2,1)S(1)}, u32[]{:S(2)}, u32[]{:S(2)}) collective-permute-start(bf16[2,4096]{1,0:T(2,128)(2,1)S(1)} %get-tuple-element.5), channel_id=1, source_target_pairs={{0,1},{1,2},{2,3},{3,4},{4,5},{5,6},{6,7},{7,8},{8,9},{9,10},{10,1... | collective-permute-start | bytes 49160 | tf_op jit(solution)/shard_map/ppermute | solution.py:26
  3.3 1.3 %collective-permute-start.1 = (bf16[2,4096]{1,0:T(2,128)(2,1)S(1)}, bf16[2,4096]{1,0:T(2,128)(2,1)S(1)}, u32[]{:S(2)}, u32[]{:S(2)}) collective-permute-start(bf16[2,4096]{1,0:T(2,128)(2,1)S(1)} %get-tuple-element.6), channel_id=1, source_target_pairs={{1,0},{2,1},{3,2},{4,3},{5,4},{6,5},{7,6},{8,7},{9,8},{10,9},{11,1... | collective-permute-start | bytes 49160 | tf_op jit(solution)/shard_map/ppermute | solution.py:27
  4.6 0.0 copy-done
  4.6 0.7 subtract_add_fusion
  5.3 0.1 copy.14
  5.4 0.1 copy.15.group_ref
  5.5 0.0 collective-permute-done
  5.5 3.0 %collective-permute-done.1 = bf16[2,4096]{1,0:T(2,128)(2,1)S(1)} collective-permute-done((bf16[2,4096]{1,0:T(2,128)(2,1)S(1)}, bf16[2,4096]{1,0:T(2,128)(2,1)S(1)}, u32[]{:S(2)}, u32[]{:S(2)}) %collective-permute-start.1) | collective-permute-done | bytes 16416 | tf_op jit(solution)/shard_map/ppermute | solution.py:27
  8.5 1.2 pad_maximum_fusion
  9.7 0.1 copy.16
  9.8 0.1 broadcast_in_dim.2.code_ref
  10.0 0.0 copy-start.1
  10.0 2.2 %copy-done.1 = bf16[64,8,4096]{2,1,0:T(8,128)(2,1)S(1)} copy-done((bf16[64,8,4096]{2,1,0:T(8,128)(2,1)S(1)}, bf16[64,8,4096]{2,1,0:T(8,128)(2,1)}, u32[]{:S(2)}) %copy-start.1) | copy-done | bytes 4194328
  12.2 24.3 %shard_map.64 = bf16[32,128,128]{2,1,0:T(8,128)(2,1)} custom-call(bf16[64,8,4096]{2,1,0:T(8,128)(2,1)S(1)} %copy-done.1, bf16[68,32,128]{2,1,0:T(8,128)(2,1)S(1)} %slice.8.p_ref, s32[64,8,128]{2,1,0:T(8,128)S(1)} %broadcast_in_dim.2.code_ref, s32[64,1,256]{2,1,0:T(1,128)S(1)} %copy.15.group_ref), custom_call_target="tpu_custom_call" | custom-call | tf_op jit(solution)/shard_map/pallas_call | solution.py:119
  36.5 0.0 copy-start.3
  36.5 0.0 copy-start.2
  36.5 8.7 %all-to-all-start = ((bf16[32,128,128]{2,1,0:T(8,128)(2,1)}), bf16[32,128,128]{2,1,0:T(8,128)(2,1)S(1)}, u32[]{:S(2)}, u32[]{:S(2)}) async-start(bf16[32,128,128]{2,1,0:T(8,128)(2,1)} %shard_map.64), calls=%async_computation | async-start | bytes 2097152 | tf_op jit(solution)/shard_map/all_to_all | solution.py:225
  45.2 0.0 copy-done.3
  45.2 0.0 copy-done.2
  45.2 0.1 reshape.34
  45.3 0.1 reshape.41
  45.4 51.8 %all-gather = s32[32,1,128]{2,1,0:T(1,128)S(1)} all-gather(s32[1,1,128]{2,1,0:T(1,128)S(1)} %reshape.41), channel_id=1, replica_groups=mesh['rows'=8,'pair'=4] {'rows','pair'}, dimensions={0}, use_global_device_ids=true | all-gather | bytes 16896 | tf_op jit(solution)/shard_map/all_gather | solution.py:224
  97.2 0.0 all-to-all-done
  97.2 5.6 %shard_map.65 = bf16[2048,128]{1,0:T(8,128)(2,1)S(1)} custom-call(s32[1,4096]{1,0:T(1,128)S(1)} %bitcast.14, bf16[4096,128]{1,0:T(8,128)(2,1)S(1)} %bitcast.12), custom_call_target="tpu_custom_call" | custom-call | tf_op jit(solution)/shard_map/pallas_call | solution.py:155
  102.8 17.9 %all_to_all.10.in_ref = bf16[32,64,128]{2,1,0:T(8,128)(2,1)} all-to-all(bf16[32,64,128]{2,1,0:T(8,128)(2,1)S(1)} %bitcast.13), channel_id=1, replica_groups=mesh['rows'=8,'pair'=4] {'rows','pair'}, dimensions={0} | all-to-all | bytes 1048576 | tf_op jit(solution)/shard_map/all_to_all | solution.py:227
  120.8 2.2 %shard_map.66 = f32[64,4096]{1,0:T(8,128)} custom-call(bf16[32,64,128]{2,1,0:T(8,128)(2,1)} %all_to_all.10.in_ref), custom_call_target="tpu_custom_call" | custom-call | tf_op jit(solution)/shard_map/pallas_call | solution.py:181
  (6 shorter events, 0.1 us)
Async XLA Ops:
  0.0 4.6 %copy-start = (s32[64,8]{0,1:T(8,128)S(1)}, s32[64,8]{0,1:T(8,128)}, u32[]{:S(2)}) copy-start(s32[64,8]{0,1:T(8,128)} %param.9) | copy-start | bytes 6148
  0.9 4.6 %collective-permute-start = (bf16[2,4096]{1,0:T(2,128)(2,1)S(1)}, bf16[2,4096]{1,0:T(2,128)(2,1)S(1)}, u32[]{:S(2)}, u32[]{:S(2)}) collective-permute-start(bf16[2,4096]{1,0:T(2,128)(2,1)S(1)} %get-tuple-element.5), channel_id=1, source_target_pairs={{0,1},{1,2},{2,3},{3,4},{4,5},{5,6},{6,7},{7,8},{8,9},{9,10},{10,1... | collective-permute-start | bytes 49160 | tf_op jit(solution)/shard_map/ppermute | solution.py:26
  3.3 5.2 %collective-permute-start.1 = (bf16[2,4096]{1,0:T(2,128)(2,1)S(1)}, bf16[2,4096]{1,0:T(2,128)(2,1)S(1)}, u32[]{:S(2)}, u32[]{:S(2)}) collective-permute-start(bf16[2,4096]{1,0:T(2,128)(2,1)S(1)} %get-tuple-element.6), channel_id=1, source_target_pairs={{1,0},{2,1},{3,2},{4,3},{5,4},{6,5},{7,6},{8,7},{9,8},{10,9},{11,1... | collective-permute-start | bytes 49160 | tf_op jit(solution)/shard_map/ppermute | solution.py:27
  10.0 2.2 %copy-start.1 = (bf16[64,8,4096]{2,1,0:T(8,128)(2,1)S(1)}, bf16[64,8,4096]{2,1,0:T(8,128)(2,1)}, u32[]{:S(2)}) copy-start(bf16[64,8,4096]{2,1,0:T(8,128)(2,1)} %a_ref.1) | copy-start | bytes 12582916
  36.5 8.7 %copy-start.3 = (s32[64]{0:T(128)S(1)}, s32[64]{0:T(128)}, u32[]{:S(2)}) copy-start(s32[64]{0:T(128)} %param.11) | copy-start | bytes 772
  36.5 8.7 %copy-start.2 = (s32[64,2]{0,1:T(2,128)S(1)}, s32[64,2]{0,1:T(2,128)}, u32[]{:S(2)}) copy-start(s32[64,2]{0,1:T(2,128)} %param.10) | copy-start | bytes 1540
  36.5 60.7 %all-to-all-start = ((bf16[32,128,128]{2,1,0:T(8,128)(2,1)}), bf16[32,128,128]{2,1,0:T(8,128)(2,1)S(1)}, u32[]{:S(2)}, u32[]{:S(2)}) async-start(bf16[32,128,128]{2,1,0:T(8,128)(2,1)} %shard_map.64), calls=%async_computation | async-start | bytes 2097152 | tf_op jit(solution)/shard_map/all_to_all | solution.py:225

commit v2 on v1

--- a/solution.py
+++ b/solution.py
@@ -140,48 +140,105 @@
     return values.reshape(rows // CHUNK, CHUNK, KS).transpose(0, 2, 1).reshape(rows * KS)
 
 
-def sum_kernel(tile_rows, target_ref, term_ref, out_ref):
-    first = pl.program_id(0) * tile_rows
-    tiles = first + iota((tile_rows, target_ref.shape[1]), 0)
-    hot = jnp.where(tiles == target_ref[...], 1.0, 0.0).astype(jnp.bfloat16)
-    out_ref[...] = jnp.dot(hot, term_ref[...], preferred_element_type=jnp.float32).astype(
-        jnp.bfloat16
-    )
-
-
-def sum_terms(targets, terms, tiles):
-    tile_rows = 256
-    count = terms.shape[0]
-    return pl.pallas_call(
-        functools.partial(sum_kernel, tile_rows),
-        grid=(tiles // tile_rows,),
-        in_specs=[
-            pl.BlockSpec((1, count), lambda g: (0, 0)),
-            pl.BlockSpec((count, LANES), lambda g: (0, 0)),
-        ],
-        out_specs=pl.BlockSpec((tile_rows, LANES), lambda g: (g, 0)),
-        out_shape=jax.ShapeDtypeStruct((tiles, LANES), jnp.bfloat16),
-        compiler_params=pltpu.CompilerParams(vmem_limit_bytes=40 * 1024 * 1024),
-    )(targets, terms)
-
-
-def join_kernel(in_ref, out_ref):
-    devices, tiles = in_ref.shape[:2]
+def exchange_kernel(rows_count, pair_count, term_ref, target_ref, out_ref, got, goals, sums, parts, sent, came, goal_sent, goal_came, sum_sent, sum_came):
+    my_row, my_pair = lax.axis_index("rows"), lax.axis_index("pair")
+    devices = rows_count * pair_count
+    me = my_row * pair_count + my_pair
+    tiles = parts.shape[1]
+    block = pair_count * tiles
+
+    def at(device):
+        return (lax.div(device, pair_count), lax.rem(device, pair_count))
+
+    def copy(src, dst, send_sem, recv_sem, device):
+        return pltpu.make_async_remote_copy(
+            src_ref=src,
+            dst_ref=dst,
+            send_sem=send_sem,
+            recv_sem=recv_sem,
+            device_id=at(device),
+            device_id_type=pl.DeviceIdType.MESH,
+        )
+
+    def term_copy(device, slot):
+        return copy(term_ref.at[device], got.at[slot], sent.at[device], came.at[slot], device)
+
+    def goal_copy(device, slot):
+        return copy(target_ref, goals.at[slot], goal_sent.at[device], goal_came.at[slot], device)
+
+    def sum_copy(device, slot):
+        rows = pl.ds(pl.multiple_of(device * tiles, tiles), tiles)
+        return copy(sums.at[rows], parts.at[slot], sum_sent.at[device], sum_came.at[slot], device)
+
+    barrier = pltpu.get_barrier_semaphore()
+    offsets = sorted(range(1, devices), key=lambda o: abs(o - devices // 2))
+    for o in offsets:
+        pl.semaphore_signal(
+            barrier, inc=1, device_id=at(lax.rem(me + o, devices)), device_id_type=pl.DeviceIdType.MESH
+        )
+    pl.semaphore_wait(barrier, devices - 1)
+
+    for o in offsets:
+        other = lax.rem(me + o, devices)
+        term_copy(other, me).start()
+        goal_copy(other, me).start()
+    got[me] = term_ref[me]
+    goals[me] = target_ref[...]
+    for o in offsets[::-1]:
+        other = lax.rem(me + o, devices)
+        goal_copy(other, other).wait_recv()
+        term_copy(other, other).wait_recv()
+
+    goal = jnp.concatenate([goals[j] for j in range(devices)], axis=1)
+    for k in sorted(range(rows_count), key=lambda o: abs(o - rows_count // 2)):
+        row = lax.rem(my_row + k, rows_count)
+        first = row * block
+        hot = jnp.where(first + iota((block, goal.shape[1]), 0) == goal, 1.0, 0.0).astype(jnp.bfloat16)
+        sums[pl.ds(pl.multiple_of(first, block), block), :] = jnp.dot(
+            hot, got[...].reshape(-1, LANES), preferred_element_type=jnp.float32
+        ).astype(jnp.bfloat16)
+        for o in range(0 if k else 1, pair_count):
+            other = row * pair_count + lax.rem(my_pair + o, pair_count)
+            sum_copy(other, me).start()
+    parts[me] = sums[pl.ds(pl.multiple_of(me * tiles, tiles), tiles), :]
+    for o in offsets:
+        other = lax.rem(me + o, devices)
+        sum_copy(other, other).wait_recv()
+
     low = iota((tiles, LANES), 1) < BLK
     half = devices * BLK
     for m in range(devices // 2):
-        one, two = in_ref[2 * m].astype(jnp.float32), in_ref[2 * m + 1].astype(jnp.float32)
-        at = m * LANES
-        out_ref[:, at : at + LANES] = jnp.where(low, one, pltpu.roll(two, BLK, 1))
-        out_ref[:, half + at : half + at + LANES] = jnp.where(low, pltpu.roll(one, BLK, 1), two)
-
-
-def join(parts):
-    devices, tiles, _ = parts.shape
+        one, two = parts[2 * m].astype(jnp.float32), parts[2 * m + 1].astype(jnp.float32)
+        to = m * LANES
+        out_ref[:, to : to + LANES] = jnp.where(low, one, pltpu.roll(two, BLK, 1))
+        out_ref[:, half + to : half + to + LANES] = jnp.where(low, pltpu.roll(one, BLK, 1), two)
+    for o in offsets:
+        other = lax.rem(me + o, devices)
+        term_copy(other, me).wait_send()
+        goal_copy(other, me).wait_send()
+        sum_copy(other, me).wait_send()
+
+
+def exchanged(terms, targets, tiles):
+    devices, count, _ = terms.shape
+    rows_count, pair_count = lax.axis_size("rows"), lax.axis_size("pair")
+    whole = pl.BlockSpec(memory_space=pltpu.VMEM)
     return pl.pallas_call(
-        join_kernel,
+        functools.partial(exchange_kernel, rows_count, pair_count),
+        in_specs=[whole, whole],
+        out_specs=whole,
         out_shape=jax.ShapeDtypeStruct((tiles, devices * LANES), jnp.float32),
-    )(parts)
+        scratch_shapes=[
+            pltpu.VMEM((devices, count, LANES), jnp.bfloat16),
+            pltpu.VMEM((devices, 1, count), jnp.int32),
+            pltpu.VMEM((devices * tiles, LANES), jnp.bfloat16),
+            pltpu.VMEM((devices, tiles, LANES), jnp.bfloat16),
+        ]
+        + [pltpu.SemaphoreType.DMA((devices,))] * 6,
+        compiler_params=pltpu.CompilerParams(
+            collective_id=0, has_side_effects=True, vmem_limit_bytes=40 * 1024 * 1024
+        ),
+    )(terms, targets)
 
 
 def routed(terms, coarse_slots, aggregate):
@@ -221,13 +278,8 @@
         return routed(terms, coarse_slots, aggregate)
     tiles = fine_rows // RATIO * KC
     targets = in_term_order(aggregate[:, None] * KC + coarse_slots)
-    targets = lax.all_gather(targets, BOTH, axis=0, tiled=True).reshape(1, -1)
-    got = lax.all_to_all(terms, BOTH, split_axis=0, concat_axis=0, tiled=True)
-    sums = sum_terms(targets, got.reshape(-1, LANES), devices * tiles)
-    parts = lax.all_to_all(
-        sums.reshape(devices, tiles, LANES), BOTH, split_axis=0, concat_axis=0, tiled=True
-    )
-    return join(parts).reshape(fine_rows // RATIO, KC, width)
+    result = exchanged(terms, targets.reshape(1, -1), tiles)
+    return result.reshape(fine_rows // RATIO, KC, width)
 
 
 def solution(mesh):

time: 123 us -> 86.2 us (0.70)
  blocking collectives: 69.7 us -> 0 us
  Pallas kernels: 32.2 us -> 72.7 us
  starting transfers between devices: 12.4 us -> 3.65 us
  waiting for transfers between devices: 2.96 us -> 1.44 us
  other arithmetic: 1.92 us -> 3.25 us
    all_gather x1 -> x0, blocking collectives: 51.8 us -> none  [body(): targets = lax.all_gather(targets, BOTH, axis=0, tiled=True).reshape(1, -1)]
    pallas_call x2 -> x1, Pallas kernels: 7.85 us -> 49.1 us  [exchanged(): pl.pallas_call(functools.partial(exchange_kernel, rows_count, pair_count)...]
    all_to_all x1 -> x0, blocking collectives: 17.9 us -> none  [body(): lax.all_to_all(sums.reshape(devices, tiles, LANES), BOTH, split_axis=0, c...]
    all_to_all x1 -> x0, starting transfers between devices: 8.71 us -> none  [body(): got = lax.all_to_all(terms, BOTH, split_axis=0, concat_axis=0, tiled=True)]
    ppermute x1, waiting for transfers between devices: 2.96 us -> 1.44 us  [extended(): after = lax.ppermute(array[:width], BOTH, down)]
    unnamed x10 -> x6, local copies, waits for them, and re-layouts: 2.4 us -> 3.27 us
  transfers between devices with their start and end apart: 3 -> 2, of which waited for: 1 -> 1; matrix products, arithmetic and copies ran while one was open for 1% -> 3% of each run, Pallas kernels for 0% -> 0%
where the time goes in v2:
time: 86.2 us; the launch traced here: 85.9 us
  Pallas kernels  72.7 us (84%)
  local copies, waits for them, and re-layouts  4.71 us (5%)
  starting transfers between devices  3.65 us (4%)
  other arithmetic  3.25 us (4%)
  waiting for transfers between devices  1.44 us (2%)
    pallas_call x1, Pallas kernels, exchanged(): pl.pallas_call(functools.partial(exchange_kernel, rows_count, pair_count)...  49.1 us
    pallas_call x1, Pallas kernels, local_terms(): pl.pallas_call(terms_kernel, grid=(steps,), in_specs=[pl.BlockSpec((CHUNK...  23.7 us
    unnamed x6, local copies, waits for them, and re-layouts  3.27 us
    ppermute x1, starting transfers between devices, extended(): before = lax.ppermute(array[length - width:], BOTH, up)  2.36 us
  transfers between devices with their start and end apart: 2, of which 1 were waited for; matrix products, arithmetic and copies ran while one was open for 3% of the time, Pallas kernels for 0%

profile of v2, /device:TPU:0, one launch (start us, length us, event | category | flops | bytes accessed | tf_op | source)
XLA Modules:
  0.0 85.9 jit_solution(8692354235185746496)
XLA Ops:
  0.0 0.0 copy-start
  0.0 0.9 %fusion = (bf16[2,4096]{1,0:T(2,128)(2,1)S(1)}, bf16[2,4096]{1,0:T(2,128)(2,1)S(1)}) fusion(bf16[64,4096]{1,0:T(8,128)(2,1)} %param.7), kind=kLoop, calls=%fused_computation.6 | loop fusion | bytes 65536 | tf_op jit(solution)/shard_map/slice | solution.py:26
  0.9 2.4 %collective-permute-start = (bf16[2,4096]{1,0:T(2,128)(2,1)S(1)}, bf16[2,4096]{1,0:T(2,128)(2,1)S(1)}, u32[]{:S(2)}, u32[]{:S(2)}) collective-permute-start(bf16[2,4096]{1,0:T(2,128)(2,1)S(1)} %get-tuple-element.5), channel_id=1, source_target_pairs={{0,1},{1,2},{2,3},{3,4},{4,5},{5,6},{6,7},{7,8},{8,9},{9,10},{10,1... | collective-permute-start | bytes 49160 | tf_op jit(solution)/shard_map/ppermute | solution.py:26
  3.3 1.3 %collective-permute-start.1 = (bf16[2,4096]{1,0:T(2,128)(2,1)S(1)}, bf16[2,4096]{1,0:T(2,128)(2,1)S(1)}, u32[]{:S(2)}, u32[]{:S(2)}) collective-permute-start(bf16[2,4096]{1,0:T(2,128)(2,1)S(1)} %get-tuple-element.6), channel_id=1, source_target_pairs={{1,0},{2,1},{3,2},{4,3},{5,4},{6,5},{7,6},{8,7},{9,8},{10,9},{11,1... | collective-permute-start | bytes 49160 | tf_op jit(solution)/shard_map/ppermute | solution.py:27
  4.6 0.7 broadcast_multiply_fusion
  5.3 0.0 copy-done
  5.3 0.7 subtract_add_fusion
  6.0 0.7 broadcast_add_fusion
  6.7 0.1 reshape.23
  6.7 0.1 reshape_reshape.3.target_ref
  6.8 0.1 copy.10
  6.9 0.1 copy.11.group_ref
  7.0 0.0 collective-permute-done
  7.0 1.4 %collective-permute-done.1 = bf16[2,4096]{1,0:T(2,128)(2,1)S(1)} collective-permute-done((bf16[2,4096]{1,0:T(2,128)(2,1)S(1)}, bf16[2,4096]{1,0:T(2,128)(2,1)S(1)}, u32[]{:S(2)}, u32[]{:S(2)}) %collective-permute-start.1) | collective-permute-done | bytes 16416 | tf_op jit(solution)/shard_map/ppermute | solution.py:27
  8.5 1.2 %pad_maximum_fusion = bf16[68,4096]{1,0:T(8,128)(2,1)S(1)} fusion(bf16[2,4096]{1,0:T(2,128)(2,1)S(1)} %collective-permute-done.1, bf16[64,4096]{1,0:T(8,128)(2,1)} %param.7, bf16[2,4096]{1,0:T(2,128)(2,1)S(1)} %collective-permute-done), kind=kLoop, calls=%fused_computation | loop fusion | flops 1671168 | bytes 1114112 | tf_op jit(solution)/shard_map/concatenate | solution.py:28
  9.7 0.1 copy.13
  9.8 0.1 broadcast_in_dim.2.code_ref
  10.0 0.0 copy-start.1
  10.0 2.2 %copy-done.1 = bf16[64,8,4096]{2,1,0:T(8,128)(2,1)S(1)} copy-done((bf16[64,8,4096]{2,1,0:T(8,128)(2,1)S(1)}, bf16[64,8,4096]{2,1,0:T(8,128)(2,1)}, u32[]{:S(2)}) %copy-start.1) | copy-done | bytes 4194328
  12.2 23.7 %shard_map.64.term_ref = bf16[32,128,128]{2,1,0:T(8,128)(2,1)S(1)} custom-call(bf16[64,8,4096]{2,1,0:T(8,128)(2,1)S(1)} %copy-done.1, bf16[68,32,128]{2,1,0:T(8,128)(2,1)S(1)} %slice.8.p_ref, s32[64,8,128]{2,1,0:T(8,128)S(1)} %broadcast_in_dim.2.code_ref, s32[64,1,256]{2,1,0:T(1,128)S(1)} %copy.11.group_ref), custom_call_target="tpu_custom_call" | custom-call | tf_op jit(solution)/shard_map/pallas_call | solution.py:119
  35.8 49.1 %shard_map.65 = f32[64,4096]{1,0:T(8,128)S(1)} custom-call(bf16[32,128,128]{2,1,0:T(8,128)(2,1)S(1)} %shard_map.64.term_ref, s32[1,128]{1,0:T(1,128)S(1)} %reshape_reshape.3.target_ref), custom_call_target="tpu_custom_call" | custom-call | tf_op jit(solution)/shard_map/pallas_call | solution.py:226
  84.9 1.0 %copy.15 = f32[4,16,4096]{2,1,0:T(8,128)} copy(f32[4,16,4096]{2,1,0:T(8,128)S(1)} %bitcast.9) | data formatting | bytes 2097152
  (4 shorter events, 0.1 us)
Async XLA Ops:
  0.0 5.3 %copy-start = (s32[64,8]{0,1:T(8,128)S(1)}, s32[64,8]{0,1:T(8,128)}, u32[]{:S(2)}) copy-start(s32[64,8]{0,1:T(8,128)} %param.9) | copy-start | bytes 6148
  0.9 6.1 %collective-permute-start = (bf16[2,4096]{1,0:T(2,128)(2,1)S(1)}, bf16[2,4096]{1,0:T(2,128)(2,1)S(1)}, u32[]{:S(2)}, u32[]{:S(2)}) collective-permute-start(bf16[2,4096]{1,0:T(2,128)(2,1)S(1)} %get-tuple-element.5), channel_id=1, source_target_pairs={{0,1},{1,2},{2,3},{3,4},{4,5},{5,6},{6,7},{7,8},{8,9},{9,10},{10,1... | collective-permute-start | bytes 49160 | tf_op jit(solution)/shard_map/ppermute | solution.py:26
  3.3 5.2 %collective-permute-start.1 = (bf16[2,4096]{1,0:T(2,128)(2,1)S(1)}, bf16[2,4096]{1,0:T(2,128)(2,1)S(1)}, u32[]{:S(2)}, u32[]{:S(2)}) collective-permute-start(bf16[2,4096]{1,0:T(2,128)(2,1)S(1)} %get-tuple-element.6), channel_id=1, source_target_pairs={{1,0},{2,1},{3,2},{4,3},{5,4},{6,5},{7,6},{8,7},{9,8},{10,9},{11,1... | collective-permute-start | bytes 49160 | tf_op jit(solution)/shard_map/ppermute | solution.py:27
  10.0 2.2 %copy-start.1 = (bf16[64,8,4096]{2,1,0:T(8,128)(2,1)S(1)}, bf16[64,8,4096]{2,1,0:T(8,128)(2,1)}, u32[]{:S(2)}) copy-start(bf16[64,8,4096]{2,1,0:T(8,128)(2,1)} %a_ref.1) | copy-start | bytes 12582916

commit v3 on v2

--- a/solution.py
+++ b/solution.py
@@ -32,89 +32,107 @@
     return lax.broadcasted_iota(jnp.int32, shape, dim)
 
 
+def put_diagonal(flat, want, low):
+    flat = flat.astype(jnp.float32)
+    turned = pltpu.roll(flat, BLK, 1)
+    zero = jnp.zeros_like(flat)
+    parts = jnp.concatenate(
+        [
+            jnp.where(low, flat, zero),
+            jnp.where(low, turned, zero),
+            jnp.where(low, zero, turned),
+            jnp.where(low, zero, flat),
+        ],
+        axis=0,
+    ).astype(jnp.bfloat16)
+    return jnp.dot(want, parts, preferred_element_type=jnp.float32).astype(jnp.bfloat16)
+
+
+def constants():
+    q = BLK // 2
+    r, k = iota((LANES, LANES), 0), iota((LANES, LANES), 1)
+    want = jnp.where(
+        (r // BLK == k // BLK) & (r % BLK == 2 * (k % q) + (k // q) % 2), 1.0, 0.0
+    ).astype(jnp.bfloat16)
+    eye = jnp.where(r == k, 1.0, 0.0).astype(jnp.bfloat16)
+    spread = jnp.where(
+        iota((q, q * KA), 0) == iota((q, q * KA), 1) // KA, 1.0, 0.0
+    ).astype(jnp.bfloat16)
+    low = iota((q, LANES), 1) < BLK
+    return want, eye, spread, low
+
+
+def row_terms(read, code, group, near, own, eye, spread, low):
+    q = BLK // 2
+    tiles = jnp.concatenate([read(c).astype(jnp.float32) for c in range(q)], axis=0)
+    codes = jnp.broadcast_to(code[None], (q,) + code.shape).reshape(tiles.shape)
+    left = jnp.concatenate(
+        [jnp.where(codes == j, tiles, 0.0).astype(jnp.bfloat16) for j in range(NEAR)], axis=1
+    )
+    products = jnp.dot(left, near, preferred_element_type=jnp.float32).astype(jnp.bfloat16)
+    turned = lax.dot_general(
+        eye, own, (((1,), (1,)), ((), ())), preferred_element_type=jnp.float32
+    ).astype(jnp.bfloat16)
+    wide = jnp.dot(turned, spread, preferred_element_type=jnp.float32)
+    rows = jnp.concatenate(
+        [jnp.where(group == s, wide, 0.0) for s in range(KS)], axis=0
+    ).astype(jnp.bfloat16)
+    full = jnp.dot(rows, products, preferred_element_type=jnp.float32)
+    terms = []
+    for s in range(KS):
+        part = full[s * LANES : (s + 1) * LANES]
+        terms.append(
+            jnp.where(low, part[:q], part[3 * q :])
+            + pltpu.roll(jnp.where(low, part[q : 2 * q], part[2 * q : 3 * q]), BLK, 1)
+        )
+    return terms
+
+
 def terms_kernel(a_ref, p_ref, code_ref, group_ref, out_ref, diag, stage):
     step = pl.program_id(0)
-    count = p_ref.shape[0]
-    q = BLK // 2
+    q = BLK // 2
+    want, eye, spread, low = constants()
 
     @pl.when(step == 0)
     def _():
-        r, k = iota((LANES, LANES), 0), iota((LANES, LANES), 1)
-        want = jnp.where(
-            (r // BLK == k // BLK) & (r % BLK == 2 * (k % q) + (k // q) % 2), 1.0, 0.0
-        ).astype(jnp.bfloat16)
-        low = iota((q, LANES), 1) < BLK
-
         def one(t, _):
-            flat = p_ref[t].astype(jnp.float32)
-            turned = pltpu.roll(flat, BLK, 1)
-            zero = jnp.zeros_like(flat)
-            parts = jnp.concatenate(
-                [
-                    jnp.where(low, flat, zero),
-                    jnp.where(low, turned, zero),
-                    jnp.where(low, zero, turned),
-                    jnp.where(low, zero, flat),
-                ],
-                axis=0,
-            ).astype(jnp.bfloat16)
-            diag[pl.ds(pl.multiple_of(t * LANES, LANES), LANES), :] = jnp.dot(
-                want, parts, preferred_element_type=jnp.float32
-            ).astype(jnp.bfloat16)
+            diag[pl.ds(pl.multiple_of(t * LANES, LANES), LANES), :] = put_diagonal(p_ref[t], want, low)
             return 0
 
-        lax.fori_loop(0, count, one, 0, unroll=4)
-
-    eye = jnp.where(iota((LANES, LANES), 0) == iota((LANES, LANES), 1), 1.0, 0.0).astype(
-        jnp.bfloat16
-    )
-    spread = jnp.where(
-        iota((q, q * KA), 0) == iota((q, q * KA), 1) // KA, 1.0, 0.0
-    ).astype(jnp.bfloat16)
-    low = iota((q, LANES), 1) < BLK
+        lax.fori_loop(0, p_ref.shape[0], one, 0, unroll=4)
 
     for i in range(CHUNK):
         row = step * CHUNK + i
-        code = code_ref[i]
-        masks = [code == j for j in range(NEAR)]
-        columns = []
-        for j in range(NEAR):
-            pieces = []
-            for c in range(q):
-                piece = a_ref[i, :, c * LANES : (c + 1) * LANES].astype(jnp.float32)
-                pieces.append(jnp.where(masks[j], piece, 0.0))
-            columns.append(jnp.concatenate(pieces, axis=0).astype(jnp.bfloat16))
-        left = jnp.concatenate(columns, axis=1)
-        near = diag[pl.ds(pl.multiple_of(row * LANES, LANES), NEAR * LANES), :]
-        products = jnp.dot(left, near, preferred_element_type=jnp.float32).astype(jnp.bfloat16)
-        own = p_ref[row + HB]
-        turned = lax.dot_general(
-            eye, own, (((1,), (1,)), ((), ())), preferred_element_type=jnp.float32
-        ).astype(jnp.bfloat16)
-        wide = jnp.dot(turned, spread, preferred_element_type=jnp.float32)
-        group = group_ref[i]
-        rows = jnp.concatenate(
-            [jnp.where(group == s, wide, 0.0) for s in range(KS)], axis=0
-        ).astype(jnp.bfloat16)
-        full = jnp.dot(rows, products, preferred_element_type=jnp.float32)
+        terms = row_terms(
+            lambda c: a_ref[i, :, c * LANES : (c + 1) * LANES],
+            code_ref[i],
+            group_ref[i],
+            diag[pl.ds(pl.multiple_of(row * LANES, LANES), NEAR * LANES), :],
+            p_ref[row + HB],
+            eye,
+            spread,
+            low,
+        )
         for s in range(KS):
-            part = full[s * LANES : (s + 1) * LANES]
-            term = jnp.where(low, part[:q], part[3 * q :]) + pltpu.roll(
-                jnp.where(low, part[q : 2 * q], part[2 * q : 3 * q]), BLK, 1
-            )
-            stage[pl.ds(s * CHUNK + i, q, stride=KS * CHUNK), :] = term
+            stage[pl.ds(s * CHUNK + i, q, stride=KS * CHUNK), :] = terms[s]
     out_ref[...] = stage[...].astype(jnp.bfloat16).reshape(out_ref.shape)
 
 
-def local_terms(a_tiles, p_tiles, a_cols, tile_group):
-    fine_rows = a_tiles.shape[0]
-    device = lax.axis_index(BOTH)
-    q = BLK // 2
-    near_p = extended(p_tiles, HB).reshape(fine_rows + 2 * HB, q, LANES)
-    own = device * fine_rows + jnp.arange(fine_rows, dtype=jnp.int32)
+def row_codes(a_cols, tile_group):
+    fine_rows = a_cols.shape[0]
+    q = BLK // 2
+    own = lax.axis_index(BOTH) * fine_rows + jnp.arange(fine_rows, dtype=jnp.int32)
     offset = a_cols - own[:, None] + HB
     code = jnp.broadcast_to(offset[:, :, None], (fine_rows, KA, LANES))
     group = jnp.tile(tile_group, (1, q)).reshape(fine_rows, 1, q * KA)
+    return code, group
+
+
+def local_terms(a_tiles, p_tiles, a_cols, tile_group):
+    fine_rows = a_tiles.shape[0]
+    q = BLK // 2
+    near_p = extended(p_tiles, HB).reshape(fine_rows + 2 * HB, q, LANES)
+    code, group = row_codes(a_cols, tile_group)
     steps = fine_rows // CHUNK
     return pl.pallas_call(
         terms_kernel,
@@ -140,7 +158,7 @@
     return values.reshape(rows // CHUNK, CHUNK, KS).transpose(0, 2, 1).reshape(rows * KS)
 
 
-def exchange_kernel(rows_count, pair_count, term_ref, target_ref, out_ref, got, goals, sums, parts, sent, came, goal_sent, goal_came, sum_sent, sum_came):
+def exchange_kernel(rows_count, pair_count, a_hbm, p_ref, code_ref, group_ref, target_ref, out_ref, a_ref, diag, stage, halo, term_ref, got, goals, sums, parts, a_came, halo_sent, halo_came, sent, came, goal_sent, goal_came, sum_sent, sum_came):
     my_row, my_pair = lax.axis_index("rows"), lax.axis_index("pair")
     devices = rows_count * pair_count
     me = my_row * pair_count + my_pair
@@ -160,8 +178,26 @@
             device_id_type=pl.DeviceIdType.MESH,
         )
 
+    fine_rows = p_ref.shape[0]
+    q = BLK // 2
+    steps = 4
+    span = fine_rows // steps
+    terms_span = span * KS
+    ahead, behind = lax.rem(me + 1, devices), lax.rem(me + devices - 1, devices)
+
+    def a_copy(step):
+        rows = pl.ds(pl.multiple_of(lax.rem(step + 1, steps) * span, span), span)
+        return pltpu.make_async_copy(a_hbm.at[rows], a_ref.at[rows], a_came.at[step])
+
     def term_copy(device, slot):
         return copy(term_ref.at[device], got.at[slot], sent.at[device], came.at[slot], device)
+
+    def term_part(device, slot, part):
+        rows = pl.ds(pl.multiple_of(part * terms_span, terms_span), terms_span)
+        return copy(term_ref.at[device, rows], got.at[slot, rows], sent.at[device], came.at[slot], device)
+
+    halo_up = copy(p_ref.at[pl.ds(fine_rows - HB, HB)], halo.at[pl.ds(0, HB)], halo_sent.at[0], halo_came.at[0], ahead)
+    halo_down = copy(p_ref.at[pl.ds(0, HB)], halo.at[pl.ds(HB, HB)], halo_sent.at[1], halo_came.at[1], behind)
 
     def goal_copy(device, slot):
         return copy(target_ref, goals.at[slot], goal_sent.at[device], goal_came.at[slot], device)
@@ -176,14 +212,64 @@
         pl.semaphore_signal(
             barrier, inc=1, device_id=at(lax.rem(me + o, devices)), device_id_type=pl.DeviceIdType.MESH
         )
+    for step in range(steps):
+        a_copy(step).start()
+    want, eye, spread, low = constants()
+
+    def own_diagonal(t, _):
+        diag[pl.ds(pl.multiple_of((t + HB) * LANES, LANES), LANES), :] = put_diagonal(p_ref[t], want, low)
+        return 0
+
+    lax.fori_loop(0, fine_rows, own_diagonal, 0, unroll=4)
     pl.semaphore_wait(barrier, devices - 1)
-
+    halo_up.start()
+    halo_down.start()
     for o in offsets:
         other = lax.rem(me + o, devices)
-        term_copy(other, me).start()
         goal_copy(other, me).start()
+    goals[me] = target_ref[...]
+
+    def quarter(step, _):
+        part = lax.rem(step + 1, steps)
+        a_copy(step).wait()
+
+        @pl.when(step == steps - 2)
+        def _():
+            halo_up.wait_recv()
+            halo_down.wait_recv()
+            for t in range(HB):
+                diag[t * LANES : (t + 1) * LANES, :] = put_diagonal(halo[t], want, low)
+                last = fine_rows + HB + t
+                diag[last * LANES : (last + 1) * LANES, :] = put_diagonal(halo[HB + t], want, low)
+
+        def chunk(c, _):
+            at_chunk = part * (span // CHUNK) + c
+
+            for i in range(CHUNK):
+                row = at_chunk * CHUNK + i
+                terms = row_terms(
+                    lambda col: a_ref[row, :, col * LANES : (col + 1) * LANES],
+                    code_ref[row],
+                    group_ref[row],
+                    diag[pl.ds(pl.multiple_of(row * LANES, LANES), NEAR * LANES), :],
+                    p_ref[row],
+                    eye,
+                    spread,
+                    low,
+                )
+                for s in range(KS):
+                    stage[pl.ds(s * CHUNK + i, q, stride=KS * CHUNK), :] = terms[s]
+            rows = pl.ds(pl.multiple_of(at_chunk * KS * CHUNK, KS * CHUNK), KS * CHUNK)
+            term_ref[:, rows, :] = stage[...].astype(jnp.bfloat16).reshape(q, KS * CHUNK, LANES)
+            return 0
+
+        lax.fori_loop(0, span // CHUNK, chunk, 0)
+        for o in offsets:
+            term_part(lax.rem(me + o, devices), me, part).start()
+        return 0
+
+    lax.fori_loop(0, steps, quarter, 0)
     got[me] = term_ref[me]
-    goals[me] = target_ref[...]
     for o in offsets[::-1]:
         other = lax.rem(me + o, devices)
         goal_copy(other, other).wait_recv()
@@ -212,6 +298,8 @@
         to = m * LANES
         out_ref[:, to : to + LANES] = jnp.where(low, one, pltpu.roll(two, BLK, 1))
         out_ref[:, half + to : half + to + LANES] = jnp.where(low, pltpu.roll(one, BLK, 1), two)
+    halo_up.wait_send()
+    halo_down.wait_send()
     for o in offsets:
         other = lax.rem(me + o, devices)
         term_copy(other, me).wait_send()
@@ -219,26 +307,37 @@
         sum_copy(other, me).wait_send()
 
 
-def exchanged(terms, targets, tiles):
-    devices, count, _ = terms.shape
+def exchanged(a_tiles, p_tiles, a_cols, tile_group, targets, tiles):
+    fine_rows = a_tiles.shape[0]
+    count, q = fine_rows * KS, BLK // 2
     rows_count, pair_count = lax.axis_size("rows"), lax.axis_size("pair")
+    devices = rows_count * pair_count
+    code, group = row_codes(a_cols, tile_group)
     whole = pl.BlockSpec(memory_space=pltpu.VMEM)
     return pl.pallas_call(
         functools.partial(exchange_kernel, rows_count, pair_count),
-        in_specs=[whole, whole],
+        in_specs=[pl.BlockSpec(memory_space=pl.ANY)] + [whole] * 4,
         out_specs=whole,
         out_shape=jax.ShapeDtypeStruct((tiles, devices * LANES), jnp.float32),
         scratch_shapes=[
+            pltpu.VMEM(a_tiles.shape, jnp.bfloat16),
+            pltpu.VMEM(((fine_rows + 2 * HB) * LANES, LANES), jnp.bfloat16),
+            pltpu.VMEM((q * KS * CHUNK, LANES), jnp.float32),
+            pltpu.VMEM((2 * HB, q, LANES), jnp.bfloat16),
+            pltpu.VMEM((devices, count, LANES), jnp.bfloat16),
             pltpu.VMEM((devices, count, LANES), jnp.bfloat16),
             pltpu.VMEM((devices, 1, count), jnp.int32),
             pltpu.VMEM((devices * tiles, LANES), jnp.bfloat16),
             pltpu.VMEM((devices, tiles, LANES), jnp.bfloat16),
+            pltpu.SemaphoreType.DMA((4,)),
+            pltpu.SemaphoreType.DMA((2,)),
+            pltpu.SemaphoreType.DMA((2,)),
         ]
         + [pltpu.SemaphoreType.DMA((devices,))] * 6,
         compiler_params=pltpu.CompilerParams(
-            collective_id=0, has_side_effects=True, vmem_limit_bytes=40 * 1024 * 1024
+            collective_id=0, has_side_effects=True, vmem_limit_bytes=48 * 1024 * 1024
         ),
-    )(terms, targets)
+    )(a_tiles, p_tiles.reshape(fine_rows, q, LANES), code, group, targets)
 
 
 def routed(terms, coarse_slots, aggregate):
@@ -273,12 +372,11 @@
 def body(a_tiles, p_tiles, a_cols, tile_group, coarse_slots, aggregate):
     fine_rows, width = p_tiles.shape
     devices = lax.axis_size(BOTH)
-    terms = local_terms(a_tiles, p_tiles, a_cols, tile_group)
     if devices * LANES != width:
-        return routed(terms, coarse_slots, aggregate)
+        return routed(local_terms(a_tiles, p_tiles, a_cols, tile_group), coarse_slots, aggregate)
+    targets = in_term_order(aggregate[:, None] * KC + coarse_slots).reshape(1, -1)
     tiles = fine_rows // RATIO * KC
-    targets = in_term_order(aggregate[:, None] * KC + coarse_slots)
-    result = exchanged(terms, targets.reshape(1, -1), tiles)
+    result = exchanged(a_tiles, p_tiles, a_cols, tile_group, targets, tiles)
     return result.reshape(fine_rows // RATIO, KC, width)
 
 

time: 86.2 us -> 59.1 us (0.69)
  Pallas kernels: 72.7 us -> 51.9 us
  starting transfers between devices: 3.65 us -> 0 us
  waiting for transfers between devices: 1.44 us -> 0 us
  other arithmetic: 3.25 us -> 2.04 us
    pallas_call x1 -> x0, Pallas kernels: 23.7 us -> none  [local_terms(): pl.pallas_call(terms_kernel, grid=(steps,), in_specs=[pl.BlockSpec((CHUNK...]
    ppermute x2 -> x0, starting transfers between devices: 3.65 us -> none  [the longest x1 2.36 us: extended(): before = lax.ppermute(array[length - width:], BOTH, up)]
    pallas_call x1, Pallas kernels: 49.1 us -> 51.9 us  [exchanged(): pl.pallas_call(functools.partial(exchange_kernel, rows_count, pair_count)...]
    ppermute x2 -> x0, waiting for transfers between devices: 1.44 us -> none  [the longest x1 1.44 us: extended(): after = lax.ppermute(array[:width], BOTH, down)]
    concatenate x1 -> x0, other arithmetic: 1.21 us -> none  [extended(): return jnp.concatenate([before, array, after], axis=0)]
    unnamed x6, local copies, waits for them, and re-layouts: 3.27 us -> 4.3 us
    slice x1 -> x0, local copies, waits for them, and re-layouts: 0.91 us -> none  [extended(): before = lax.ppermute(array[length - width:], BOTH, up)]
  transfers between devices with their start and end apart: 2 -> 0, of which waited for: 1 -> 0; matrix products, arithmetic and copies ran while one was open for 3% -> 0% of each run, Pallas kernels for 0% -> 0%
where the time goes in v3:
time: 59.1 us; the launch traced here: 58.8 us
  Pallas kernels  51.9 us (88%)
  local copies, waits for them, and re-layouts  4.79 us (8%)
  other arithmetic  2.04 us (3%)
    pallas_call x1, Pallas kernels, exchanged(): pl.pallas_call(functools.partial(exchange_kernel, rows_count, pair_count)...  51.9 us
    unnamed x6, local copies, waits for them, and re-layouts  4.3 us

profile of v3, /device:TPU:0, one launch (start us, length us, event | category | flops | bytes accessed | tf_op | source)
XLA Modules:
  0.0 58.8 jit_solution(15542800358906674707)
XLA Ops:
  0.0 0.0 copy-start
  0.0 0.7 %broadcast_multiply_fusion = s32[64]{0:T(128)S(1)} fusion(s32[64]{0:T(128)} %param.11), kind=kLoop, calls=%fused_computation.4 | loop fusion | flops 64 | bytes 512 | tf_op jit(solution)/shard_map/mul | solution.py:377
  0.7 0.7 %broadcast_add_fusion = s32[64,2]{0,1:T(2,128)S(1)} fusion(s32[64,2]{0,1:T(2,128)} %param.10, s32[64]{0:T(128)S(1)} %broadcast_multiply_fusion), kind=kLoop, calls=%fused_computation.2 | loop fusion | flops 128 | bytes 1280 | tf_op jit(solution)/shard_map/add | solution.py:377
  1.4 0.7 %subtract_add_fusion = s32[64,8]{0,1:T(8,128)S(1)} fusion(s32[64,8]{0,1:T(8,128)} %param.8, s32[64]{0:T(128)S(1)} %iota_add_fusion), kind=kLoop, calls=%fused_computation.1 | loop fusion | flops 1024 | bytes 4352 | tf_op jit(solution)/shard_map/add | solution.py:125
  2.0 0.1 reshape.23
  2.1 0.1 reshape_reshape.3.target_ref
  2.2 0.1 copy.10
  2.3 0.0 copy-done
  2.3 0.1 copy.12.group_ref
  2.4 0.1 broadcast_in_dim.2.code_ref
  2.6 1.1 %copy.13 = bf16[8,8,32,128]{3,2,1,0:T(8,128)(2,1)S(1)} copy(bf16[8,8,32,128]{3,1,2,0:T(8,128)(2,1)} %bitcast.10) | data formatting | bytes 1048576
  3.7 0.0 copy-start.1
  3.7 2.2 %copy-done.1 = bf16[64,8,4096]{2,1,0:T(8,128)(2,1)S(1)} copy-done((bf16[64,8,4096]{2,1,0:T(8,128)(2,1)S(1)}, bf16[64,8,4096]{2,1,0:T(8,128)(2,1)}, u32[]{:S(2)}) %copy-start.1) | copy-done | bytes 4194328
  5.9 51.9 %shard_map.64 = f32[64,4096]{1,0:T(8,128)S(1)} custom-call(bf16[64,8,4096]{2,1,0:T(8,128)(2,1)S(1)} %copy-done.1, bf16[64,32,128]{2,1,0:T(8,128)(2,1)S(1)} %bitcast.9, s32[64,8,128]{2,1,0:T(8,128)S(1)} %broadcast_in_dim.2.code_ref, s32[64,1,256]{2,1,0:T(1,128)S(1)} %copy.12.group_ref, s32[1,128]{1,0:T(1,128)S(1)} %reshape_reshape.3.target_ref), custom_call_target="tpu_custom_call" | custom-call | tf_op jit(solution)/shard_map/pallas_call | solution.py:317
  57.8 1.0 %copy.15 = f32[4,16,4096]{2,1,0:T(8,128)} copy(f32[4,16,4096]{2,1,0:T(8,128)S(1)} %bitcast.8) | data formatting | bytes 2097152
  (3 shorter events, 0.0 us)
Async XLA Ops:
  0.0 2.3 %copy-start = (s32[64,8]{0,1:T(8,128)S(1)}, s32[64,8]{0,1:T(8,128)}, u32[]{:S(2)}) copy-start(s32[64,8]{0,1:T(8,128)} %param.9) | copy-start | bytes 6148
  3.7 2.2 %copy-start.1 = (bf16[64,8,4096]{2,1,0:T(8,128)(2,1)S(1)}, bf16[64,8,4096]{2,1,0:T(8,128)(2,1)}, u32[]{:S(2)}) copy-start(bf16[64,8,4096]{2,1,0:T(8,128)(2,1)} %a_hbm.1) | copy-start | bytes 12582916

commit v4 on v3

--- a/solution.py
+++ b/solution.py
@@ -16,6 +16,7 @@
 LANES = 128
 NEAR = 2 * HB + 1
 CHUNK = 8
+STEPS = 8
 BOTH = ("rows", "pair")
 
 
@@ -65,18 +66,22 @@
 def row_terms(read, code, group, near, own, eye, spread, low):
     q = BLK // 2
     tiles = jnp.concatenate([read(c).astype(jnp.float32) for c in range(q)], axis=0)
-    codes = jnp.broadcast_to(code[None], (q,) + code.shape).reshape(tiles.shape)
-    left = jnp.concatenate(
-        [jnp.where(codes == j, tiles, 0.0).astype(jnp.bfloat16) for j in range(NEAR)], axis=1
-    )
+    tiles = tiles.astype(jnp.bfloat16)
+
+    def picked(j):
+        one = jnp.where(code == j, 1.0, 0.0)
+        pair = jnp.concatenate([one, one], axis=0).astype(jnp.bfloat16)
+        return jnp.broadcast_to(pair[None], (q // 2,) + pair.shape).reshape(tiles.shape)
+
+    left = jnp.concatenate([tiles * picked(j) for j in range(NEAR)], axis=1)
     products = jnp.dot(left, near, preferred_element_type=jnp.float32).astype(jnp.bfloat16)
     turned = lax.dot_general(
         eye, own, (((1,), (1,)), ((), ())), preferred_element_type=jnp.float32
     ).astype(jnp.bfloat16)
-    wide = jnp.dot(turned, spread, preferred_element_type=jnp.float32)
+    wide = jnp.dot(turned, spread, preferred_element_type=jnp.float32).astype(jnp.bfloat16)
     rows = jnp.concatenate(
-        [jnp.where(group == s, wide, 0.0) for s in range(KS)], axis=0
-    ).astype(jnp.bfloat16)
+        [wide * jnp.where(group == s, 1.0, 0.0).astype(jnp.bfloat16) for s in range(KS)], axis=0
+    )
     full = jnp.dot(rows, products, preferred_element_type=jnp.float32)
     terms = []
     for s in range(KS):
@@ -180,7 +185,7 @@
 
     fine_rows = p_ref.shape[0]
     q = BLK // 2
-    steps = 4
+    steps = STEPS
     span = fine_rows // steps
     terms_span = span * KS
     ahead, behind = lax.rem(me + 1, devices), lax.rem(me + devices - 1, devices)
@@ -316,7 +321,7 @@
     whole = pl.BlockSpec(memory_space=pltpu.VMEM)
     return pl.pallas_call(
         functools.partial(exchange_kernel, rows_count, pair_count),
-        in_specs=[pl.BlockSpec(memory_space=pl.ANY)] + [whole] * 4,
+        in_specs=[pl.BlockSpec(memory_space=pltpu.HBM)] + [whole] * 4,
         out_specs=whole,
         out_shape=jax.ShapeDtypeStruct((tiles, devices * LANES), jnp.float32),
         scratch_shapes=[
@@ -329,7 +334,7 @@
             pltpu.VMEM((devices, 1, count), jnp.int32),
             pltpu.VMEM((devices * tiles, LANES), jnp.bfloat16),
             pltpu.VMEM((devices, tiles, LANES), jnp.bfloat16),
-            pltpu.SemaphoreType.DMA((4,)),
+            pltpu.SemaphoreType.DMA((STEPS,)),
             pltpu.SemaphoreType.DMA((2,)),
             pltpu.SemaphoreType.DMA((2,)),
         ]

time: 59.1 us -> 57 us (0.964)
  Pallas kernels: 51.9 us -> 49.8 us
    pallas_call x1, Pallas kernels: 51.9 us -> 49.8 us  [exchanged(): pl.pallas_call(functools.partial(exchange_kernel, rows_count, pair_count)...]
where the time goes in v4:
time: 57 us; the launch traced here: 56.7 us
  Pallas kernels  49.8 us (87%)
  local copies, waits for them, and re-layouts  4.79 us (8%)
  other arithmetic  2.04 us (4%)
    pallas_call x1, Pallas kernels, exchanged(): pl.pallas_call(functools.partial(exchange_kernel, rows_count, pair_count)...  49.8 us
    unnamed x6, local copies, waits for them, and re-layouts  4.3 us

profile of v4, /device:TPU:0, one launch (start us, length us, event | category | flops | bytes accessed | tf_op | source)
XLA Modules:
  0.0 56.7 jit_solution(3270370383290941949)
XLA Ops:
  0.0 0.0 copy-start
  0.0 0.7 %broadcast_multiply_fusion = s32[64]{0:T(128)S(1)} fusion(s32[64]{0:T(128)} %param.11), kind=kLoop, calls=%fused_computation.4 | loop fusion | flops 64 | bytes 512 | tf_op jit(solution)/shard_map/mul | solution.py:382
  0.7 0.7 %broadcast_add_fusion = s32[64,2]{0,1:T(2,128)S(1)} fusion(s32[64,2]{0,1:T(2,128)} %param.10, s32[64]{0:T(128)S(1)} %broadcast_multiply_fusion), kind=kLoop, calls=%fused_computation.2 | loop fusion | flops 128 | bytes 1280 | tf_op jit(solution)/shard_map/add | solution.py:382
  1.4 0.7 %subtract_add_fusion = s32[64,8]{0,1:T(8,128)S(1)} fusion(s32[64,8]{0,1:T(8,128)} %param.8, s32[64]{0:T(128)S(1)} %iota_add_fusion), kind=kLoop, calls=%fused_computation.1 | loop fusion | flops 1024 | bytes 4352 | tf_op jit(solution)/shard_map/add | solution.py:130
  2.0 0.1 reshape.23
  2.1 0.1 reshape_reshape.3.target_ref
  2.2 0.1 copy.10
  2.3 0.0 copy-done
  2.3 0.1 copy.12.group_ref
  2.4 0.1 broadcast_in_dim.2.code_ref
  2.6 1.1 %copy.13 = bf16[8,8,32,128]{3,2,1,0:T(8,128)(2,1)S(1)} copy(bf16[8,8,32,128]{3,1,2,0:T(8,128)(2,1)} %bitcast.10) | data formatting | bytes 1048576
  3.7 0.0 copy-start.1
  3.7 2.2 %copy-done.1 = bf16[64,8,4096]{2,1,0:T(8,128)(2,1)S(1)} copy-done((bf16[64,8,4096]{2,1,0:T(8,128)(2,1)S(1)}, bf16[64,8,4096]{2,1,0:T(8,128)(2,1)}, u32[]{:S(2)}) %copy-start.1) | copy-done | bytes 4194328
  5.9 49.8 %shard_map.64 = f32[64,4096]{1,0:T(8,128)S(1)} custom-call(bf16[64,8,4096]{2,1,0:T(8,128)(2,1)S(1)} %copy-done.1, bf16[64,32,128]{2,1,0:T(8,128)(2,1)S(1)} %bitcast.9, s32[64,8,128]{2,1,0:T(8,128)S(1)} %broadcast_in_dim.2.code_ref, s32[64,1,256]{2,1,0:T(1,128)S(1)} %copy.12.group_ref, s32[1,128]{1,0:T(1,128)S(1)} %reshape_reshape.3.target_ref), custom_call_target="tpu_custom_call" | custom-call | tf_op jit(solution)/shard_map/pallas_call | solution.py:322
  55.7 1.0 %copy.15 = f32[4,16,4096]{2,1,0:T(8,128)} copy(f32[4,16,4096]{2,1,0:T(8,128)S(1)} %bitcast.8) | data formatting | bytes 2097152
  (3 shorter events, 0.0 us)
Async XLA Ops:
  0.0 2.3 %copy-start = (s32[64,8]{0,1:T(8,128)S(1)}, s32[64,8]{0,1:T(8,128)}, u32[]{:S(2)}) copy-start(s32[64,8]{0,1:T(8,128)} %param.9) | copy-start | bytes 6148
  3.7 2.2 %copy-start.1 = (bf16[64,8,4096]{2,1,0:T(8,128)(2,1)S(1)}, bf16[64,8,4096]{2,1,0:T(8,128)(2,1)}, u32[]{:S(2)}) copy-start(bf16[64,8,4096]{2,1,0:T(8,128)(2,1)} %a_hbm.1) | copy-start | bytes 12582916
